TPU v7x, 32 devices: a whole 2x2x4 slice. The times are simulated.
32 devices in a mesh: groups: 2 (over x), blk: 16 (over z, y, core).
Axes of the slice: x: 2, y: 2, z: 4, core: 2. Of those that a mesh axis runs over, the one named last changes fastest.
Arguments:
- train_acts: bfloat16 [4096, 768], P(('groups', 'blk')), parts along dimension 0, may hold values from -6 to 6
- train_grads: bfloat16 [4096, 2048], P(('groups', 'blk')), parts along dimension 0, may hold values from -0.059814453 to 0.059814453
- train_expert: int32 [4096, 1], P(('groups', 'blk')), parts along dimension 0, may hold values from 0 to 1; in each aligned block of 128 rows (0 to 127, 128 to 255, ...) at most 96 rows name the same one
- train_doc: int32 [4096], P(('groups', 'blk')), parts along dimension 0, may hold values from 0 to 3
- query_acts: bfloat16 [64, 768], P('blk'), may hold values from -6 to 6
- query_grads: bfloat16 [64, 2048], P('blk'), may hold values from -0.059814453 to 0.059814453
- query_expert: int32 [64, 1], P('blk'), may hold values from 0 to 1; in each aligned block of 4 rows (0 to 3, 4 to 7, ...) at most 3 rows name the same one
- query_ids: int32 [64], P('blk'), may hold values from 0 to 1
- basis_out: bfloat16 [2, 2048, 2048], P(None, None, 'blk'), may hold values from -0.125 to 0.125
- basis_in: bfloat16 [2, 768, 768], P(None, None, 'blk'), may hold values from -0.21875 to 0.21875
- eigenvalues: bfloat16 [2, 2048, 768], P(None, 'blk'), may hold values from 0.019897461 to 5
Outputs:
- scores: float32 [128, 32], P(('groups', 'blk')), parts along dimension 0
There are 2 independent parts, one for each index of `groups`. A program takes and returns all parts, laid end to end along the dimension named above; an argument that names none is the same for every part. Nothing has to cross between parts.
Inputs may be any that keep to these rules, and one draw needn't show every extreme that they name: `train_expert`: the rows of one device name each expert at most 96 times; in every draw some device's rows name one expert exactly 96 times. `query_expert`: the rows of one device name each expert at most 3 times; in every draw some device's rows name one expert exactly 3 times.
All inputs are finite; a program needn't handle non-finite values.
Results may differ from a plain program's by a relative error of at most 0.0053.
Values may be sent and summed in bfloat16 or wider, within the bound.
A program may use at most 128 MiB of HBM per device.

v0:
```python
import jax
import jax.numpy as jnp
from jax import lax
from jax.sharding import PartitionSpec as P

DOCS_DEV = 4
QRY_DEV = 2
CAP = 96
QCAP = 3
DAMPING = 0.05


def slot_table(experts, capacity, count):
    rows = experts.shape[0]
    onehot = (experts[:, None] == jnp.arange(count, dtype=jnp.int32)[None, :]).astype(jnp.int32)
    before = jnp.cumsum(onehot, axis=0) - onehot
    rank = jnp.sum(before * onehot, axis=1)
    target = experts * capacity + rank
    source = (
        jnp.zeros((count * capacity,), jnp.int32).at[target].set(jnp.arange(rows, dtype=jnp.int32))
    )
    filled = jnp.zeros((count * capacity,), jnp.int32).at[target].set(1)
    return (source.reshape(count, capacity), filled.reshape(count, capacity))


def turner(rows, piece):
    return jnp.einsum("ecd,edn->ecn", rows, piece, preferred_element_type=jnp.float32)


def body(
    train_acts,
    train_grads,
    train_expert,
    train_doc,
    query_acts,
    query_grads,
    query_expert,
    query_ids,
    basis_out,
    basis_in,
    eigenvalues,
):
    count = basis_out.shape[0]
    train_src, train_fill = slot_table(train_expert[:, 0], CAP, count)
    query_src, query_fill = slot_table(query_expert[:, 0], QCAP, count)
    source = jnp.concatenate([train_src, query_src + train_acts.shape[0]], axis=1)
    filled = jnp.concatenate([train_fill, query_fill], axis=1)
    weight = filled.astype(jnp.bfloat16)[:, :, None]
    grads_in = jnp.concatenate([train_grads, query_grads], axis=0)[source] * weight
    acts_in = jnp.concatenate([train_acts, query_acts], axis=0)[source] * weight
    slot_doc = train_doc[train_src]
    queries_total = QRY_DEV * lax.axis_size("blk")
    global_ids = jnp.where(
        query_fill == 1, lax.axis_index("blk") * QRY_DEV + query_ids[query_src], -1
    )
    rot_grads = turner(grads_in, lax.all_gather(basis_out, "blk", axis=2, tiled=True))
    rot_acts = turner(acts_in, lax.all_gather(basis_in, "blk", axis=2, tiled=True))
    rot_grads = rot_grads.astype(jnp.bfloat16)
    rot_acts = rot_acts.astype(jnp.bfloat16)
    train_g = rot_grads[:, :CAP]
    train_a = rot_acts[:, :CAP]
    query_g = rot_grads[:, CAP:]
    query_a = rot_acts[:, CAP:]
    doc_masks = [
        ((slot_doc == doc) & (train_fill == 1)).astype(jnp.bfloat16) for doc in range(DOCS_DEV)
    ]
    scale = lax.all_gather(eigenvalues, "blk", axis=1, tiled=True).astype(jnp.float32) + DAMPING
    mats = []
    for mask in doc_masks:
        summed = jnp.einsum(
            "ecn,ecf->enf", train_g * mask[:, :, None], train_a, preferred_element_type=jnp.float32
        )
        mats.append((summed / scale).astype(jnp.bfloat16))
    doc_mats = jnp.stack(mats)
    piece_g, piece_a, piece_ids = lax.all_gather(
        (query_g, query_a, global_ids), "blk", axis=1, tiled=True
    )
    image = jnp.einsum("esf,kedf->kesd", piece_a, doc_mats, preferred_element_type=jnp.float32)
    token = jnp.einsum("kesd,esd->esk", image, piece_g.astype(jnp.float32))
    table = (
        piece_ids.reshape(-1)[:, None] == jnp.arange(queries_total, dtype=jnp.int32)[None, :]
    ).astype(jnp.float32)
    return jnp.dot(token.reshape(-1, DOCS_DEV).T, table, precision=lax.Precision.HIGHEST)


def solution(mesh):
    in_specs = (
        P(("groups", "blk"), None),
        P(("groups", "blk"), None),
        P(("groups", "blk"), None),
        P(("groups", "blk")),
        P("blk", None),
        P("blk", None),
        P("blk", None),
        P("blk"),
        P(None, None, "blk"),
        P(None, None, "blk"),
        P(None, "blk", None),
    )
    out_specs = P(("groups", "blk"), None)
    return jax.shard_map(body, mesh=mesh, in_specs=in_specs, out_specs=out_specs, check_vma=False)
```

profile of v0, /device:TPU:0, one launch (start us, length us, event | category | flops | bytes accessed | tf_op | source)
XLA Modules:
  0.0 286.9 jit_solution(85553088531195338)
XLA Ops:
  6.5 0.7 all-gather.7.cloned.1.call-update
  7.3 0.7 all-gather.5.cloned.1.call-update
  8.1 0.7 all-gather.9.cloned.1.call-update
  8.8 0.7 fusion.36
  9.6 0.7 select_reduce_fusion.1
  10.3 0.7 fusion.38
  11.7 0.6 scatter_custom_fusion.3
  12.3 1.3 gather_fusion.3
  13.7 0.7 fusion.33
  14.6 0.8 select_reduce_fusion
  15.5 0.7 fusion.37
  16.1 1.0 scatter_custom_fusion.2
  17.2 1.0 scatter_custom_fusion
  18.5 1.1 pad_maximum_fusion.1
  19.7 1.2 gather_fusion
  21.1 1.0 gather_fusion.2
  22.3 1.6 gather_fusion.1
  24.3 23.1 %all-gather = s32[16,3,2]{1,2,0:T(2,128)S(1)} all-gather(s32[1,3,2]{1,2,0:T(2,128)S(1)} %bitcast.49), channel_id=1, replica_groups=mesh['groups'=2,'blk'=16] {'blk'}, dimensions={0}, use_global_device_ids=true | all-gather | bytes 408 | tf_op jit(solution)/shard_map/all_gather | solution.py:75
  47.6 7.1 %all-gather.7.cloned.1.call-done = bf16[2,768,768]{1,2,0:T(8,128)(2,1)} async-done(((bf16[2,768,48]{1,2,0:T(8,128)(2,1)}), bf16[2,768,768]{1,2,0:T(8,128)(2,1)}) %all-gather.7.cloned.1.call-update) | async-done | bytes 2359312 | tf_op jit(solution)/shard_map/all_gather | solution.py:57
  54.8 2.5 convolution_convert_fusion.1
  57.3 20.2 %all_gather.21 = bf16[2,48,768]{2,0,1:T(2,128)(2,1)S(1)} all-gather(bf16[2,3,768]{2,0,1:T(2,128)(2,1)S(1)} %copy.20), channel_id=1, replica_groups=mesh['groups'=2,'blk'=16] {'blk'}, dimensions={1}, use_global_device_ids=true | all-gather | bytes 156672 | tf_op jit(solution)/shard_map/all_gather | solution.py:75
  77.5 109.2 %all-gather.5.cloned.1.call-done = bf16[2,2048,2048]{2,1,0:T(8,128)(2,1)} async-done(((bf16[2,2048,128]{2,1,0:T(8,128)(2,1)}), bf16[2,2048,2048]{2,1,0:T(8,128)(2,1)}) %all-gather.5.cloned.1.call-update) | async-done | bytes 16777232 | tf_op jit(solution)/shard_map/all_gather | solution.py:56
  186.7 8.5 %convolution_convert_fusion = bf16[2,99,2048]{2,1,0:T(8,128)(2,1)S(1)} fusion(bf16[2,2048,2048]{2,1,0:T(8,128)(2,1)} %all-gather.5.cloned.1.call-done, bf16[2,99,2048]{2,1,0:T(8,128)(2,1)S(1)} %reshape.209, bf16[2,99]{1,0:T(2,128)(2,1)S(1)} %pad_maximum_fusion.3), kind=kOutput, calls=%fused_computation.23 | convolution fusion | flops 1661755392 | bytes 18399628 | tf_op jit(solution)/shard_map/ecd,edn->ecn/dot_general | solution.py:27
  195.2 22.0 %all_gather.22 = bf16[2,48,2048]{2,0,1:T(2,128)(2,1)S(1)} all-gather(bf16[2,3,2048]{2,0,1:T(2,128)(2,1)S(1)} %copy.23), channel_id=1, replica_groups=mesh['groups'=2,'blk'=16] {'blk'}, dimensions={1}, use_global_device_ids=true | all-gather | bytes 417792 | tf_op jit(solution)/shard_map/all_gather | solution.py:75
  217.2 33.7 %all-gather.9.cloned.1.call-done = bf16[2,2048,768]{2,1,0:T(8,128)(2,1)} async-done(((bf16[2,128,768]{2,1,0:T(8,128)(2,1)}), bf16[2,2048,768]{2,1,0:T(8,128)(2,1)}) %all-gather.9.cloned.1.call-update) | async-done | bytes 6291472 | tf_op jit(solution)/shard_map/all_gather | solution.py:67
  250.9 4.9 %fusion.3 = bf16[1,2,2048,768]{3,2,1,0:T(8,128)(2,1)S(1)} fusion(bf16[2,2048,768]{2,1,0:T(8,128)(2,1)} %all-gather.9.cloned.1.call-done, bf16[2,99,2048]{2,1,0:T(8,128)(2,1)S(1)} %convolution_convert_fusion, bf16[2,96]{1,0:T(2,128)(2,1)S(1)} %reshape.293, bf16[2,99,768]{2,1,0:T(8,128)(2,1)S(1)} %convolution_convert_fusion.1), kind=kOutput, calls=%fused_computation.17 | convolution fusion | flops 616955904 | bytes 13664768 | tf_op jit(solution)/shard_map/ecn,ecf->enf/dot_general | solution.py:70
  255.8 2.5 fusion.4
  258.3 4.2 %fusion.5 = bf16[1,2,2048,768]{3,2,1,0:T(8,128)(2,1)} fusion(bf16[2,2048,768]{2,1,0:T(8,128)(2,1)S(1)} %copy-done.3, bf16[2,99,2048]{2,1,0:T(8,128)(2,1)S(1)} %convolution_convert_fusion, bf16[2,96]{1,0:T(2,128)(2,1)S(1)} %reshape.295, bf16[2,99,768]{2,1,0:T(8,128)(2,1)S(1)} %convolution_convert_fusion.1), kind=kOutput, calls=%fused_computation.19 | convolution fusion | flops 616955904 | bytes 13664768 | tf_op jit(solution)/shard_map/ecn,ecf->enf/dot_general | solution.py:70
  262.4 4.1 %fusion.2 = bf16[1,2,2048,768]{3,2,1,0:T(8,128)(2,1)} fusion(bf16[2,2048,768]{2,1,0:T(8,128)(2,1)S(1)} %copy-done.3, bf16[2,99,2048]{2,1,0:T(8,128)(2,1)S(1)} %convolution_convert_fusion, bf16[2,96]{1,0:T(2,128)(2,1)S(1)} %reshape.292, bf16[2,99,768]{2,1,0:T(8,128)(2,1)S(1)} %convolution_convert_fusion.1), kind=kOutput, calls=%fused_computation.16 | convolution fusion | flops 616955904 | bytes 13664768 | tf_op jit(solution)/shard_map/ecn,ecf->enf/dot_general | solution.py:70
  266.5 10.9 %fusion.8 = bf16[4,2,48,2048]{3,2,0,1:T(8,128)(2,1)S(1)} fusion(bf16[2,48,768,1]{2,0,1,3:T(2,128)(2,1)S(1)} %bitcast.46, bf16[1,2,2048,768]{3,2,1,0:T(8,128)(2,1)} %fusion.5, bf16[1,2,2048,768]{3,2,1,0:T(8,128)(2,1)S(1)} %fusion.4, bf16[1,2,2048,768]{3,2,1,0:T(8,128)(2,1)S(1)} %fusion.3, bf16[1,2,2048,768]{3,2,1,0:T(8,128)(2,1)} %fusion.2), kind=kOutput, calls=%fused_computation.22 | convolution fusion | flops 1245708288 | bytes 26886144 | tf_op jit(solution)/shard_map/esf,kedf->kesd/dot_general | solution.py:78
  277.4 2.2 fusion.6
  279.6 0.8 fusion.34
  (53 shorter events, 2.8 us)
Async XLA Ops:
  6.5 15.7 %copy-start = (s32[128]{0:T(128)S(1)}, s32[128]{0:T(128)}, u32[]{:S(2)}) copy-start(s32[128]{0:T(128)} %param.14) | copy-start | bytes 1540
  6.5 48.2 %all-gather.7.cloned.1.call-start = ((), (), s32[]{:S(2)}) async-start(), calls=%async_computation.1 | async-start | bytes 2506752 | tf_op jit(solution)/shard_map/all_gather | solution.py:57
  7.3 179.4 %all-gather.5.cloned.1.call-start = ((), (), s32[]{:S(2)}) async-start(), calls=%async_computation | async-start | bytes 17825792 | tf_op jit(solution)/shard_map/all_gather | solution.py:56
  8.0 13.0 %copy-start.1 = (bf16[128,768]{1,0:T(8,128)(2,1)S(1)}, bf16[128,768]{1,0:T(8,128)(2,1)}, u32[]{:S(2)}) copy-start(bf16[128,768]{1,0:T(8,128)(2,1)} %param.11) | copy-start | bytes 589828
  8.0 13.0 %copy-start.2 = (bf16[4,768]{1,0:T(4,128)(2,1)S(1)}, bf16[4,768]{1,0:T(4,128)(2,1)}, u32[]{:S(2)}) copy-start(bf16[4,768]{1,0:T(4,128)(2,1)} %param.15) | copy-start | bytes 18436
  8.0 242.9 %all-gather.9.cloned.1.call-start = ((), (), s32[]{:S(2)}) async-start(), calls=%async_computation.2 | async-start | bytes 6684672 | tf_op jit(solution)/shard_map/all_gather | solution.py:67
  250.9 4.9 %copy-start.3 = (bf16[2,2048,768]{2,1,0:T(8,128)(2,1)S(1)}, bf16[2,2048,768]{2,1,0:T(8,128)(2,1)}, u32[]{:S(2)}) copy-start(bf16[2,2048,768]{2,1,0:T(8,128)(2,1)} %all-gather.9.cloned.1.call-done) | copy-start | bytes 18874372
Sparse Core Ops, SparseCore 0:
  9.6 45.0 all-gather.6
  56.9 129.7 all-gather.4
  189.0 61.8 all-gather.8
where the time goes:
time: 287 us
  waiting for transfers between devices  152 us (53%)
  blocking collectives  65.3 us (23%)
  matrix products  40.5 us (14%)
  between operations  13.4 us (5%)
  local copies, waits for them, and re-layouts  9.76 us (3%)
  other arithmetic  5.92 us (2%)
    all_gather x1, waiting for transfers between devices, body(): lax.all_gather(basis_out, 'blk', axis=2, tiled=True)  109 us
    all_gather x3, blocking collectives, body(): lax.all_gather((query_g, query_a, global_ids), 'blk', axis=1, tiled=True)  65.3 us
    all_gather x1, waiting for transfers between devices, body(): lax.all_gather(eigenvalues, 'blk', axis=1, tiled=True).astype(jnp.float32)  33.7 us
    dot_general x4, matrix products, body(): jnp.einsum('ecn,ecf->enf', train_g * mask[:, :, None], train_a, preferred...  15.6 us
    dot_general x2, matrix products, turner(): jnp.einsum('ecd,edn->ecn', rows, piece, preferred_element_type=jnp.float32)  11 us
    dot_general x1, matrix products, body(): jnp.einsum('esf,kedf->kesd', piece_a, doc_mats, preferred_element_type=jn...  10.9 us
    all_gather x1, waiting for transfers between devices, body(): lax.all_gather(basis_in, 'blk', axis=2, tiled=True)  7.12 us
  transfers between devices with their start and end apart: 3, of which 3 were waited for; matrix products, arithmetic and copies ran while one was open for 9% of the time, Pallas kernels for 0%

commit v1 on v0

--- a/solution.py
+++ b/solution.py
@@ -8,6 +8,27 @@
 CAP = 96
 QCAP = 3
 DAMPING = 0.05
+
+
+def collect(value, axis, dim):
+    size, place, span = (lax.axis_size(axis), lax.axis_index(axis), value.shape[dim])
+    right = [(i, (i + 1) % size) for i in range(size)]
+    backward = [(i, (i - 1) % size) for i in range(size)]
+    out = jnp.zeros((*value.shape[:dim], size * span, *value.shape[dim + 1 :]), value.dtype)
+    out = lax.dynamic_update_slice_in_dim(out, value, place * span, axis=dim)
+    from_left = from_right = value
+    halfway = size // 2
+    for step in range(1, halfway + 1):
+        from_left = lax.ppermute(from_left, axis, right)
+        out = lax.dynamic_update_slice_in_dim(
+            out, from_left, (place - step) % size * span, axis=dim
+        )
+        if step < size - halfway:
+            from_right = lax.ppermute(from_right, axis, backward)
+            out = lax.dynamic_update_slice_in_dim(
+                out, from_right, (place + step) % size * span, axis=dim
+            )
+    return out
 
 
 def slot_table(experts, capacity, count):
@@ -64,7 +85,7 @@
     doc_masks = [
         ((slot_doc == doc) & (train_fill == 1)).astype(jnp.bfloat16) for doc in range(DOCS_DEV)
     ]
-    scale = lax.all_gather(eigenvalues, "blk", axis=1, tiled=True).astype(jnp.float32) + DAMPING
+    scale = collect(eigenvalues, "blk", 1).astype(jnp.float32) + DAMPING
     mats = []
     for mask in doc_masks:
         summed = jnp.einsum(

time: 287 us -> 275 us (0.958)
  waiting for transfers between devices: 152 us -> 92.9 us
  starting transfers between devices: 0.08 us -> 29.5 us
  local copies, waits for them, and re-layouts: 9.76 us -> 29.5 us
  blocking collectives: 65.3 us -> 62.4 us
    all_gather x1, waiting for transfers between devices: 109 us -> 38.2 us  [body(): lax.all_gather(basis_out, 'blk', axis=2, tiled=True)]
    ppermute x0 -> x15, waiting for transfers between devices: none -> 53.3 us  [the longest x8 28.7 us: collect(): from_left = lax.ppermute(from_left, axis, right)]
    all_gather x1 -> x0, waiting for transfers between devices: 33.7 us -> none  [body(): lax.all_gather(eigenvalues, 'blk', axis=1, tiled=True).astype(jnp.float32)]
    ppermute x0 -> x15, starting transfers between devices: none -> 29.4 us  [the longest x7 28.9 us: collect(): from_right = lax.ppermute(from_right, axis, backward)]
    dynamic_update_slice x0 -> x16, local copies, waits for them, and re-layouts: none -> 16.7 us  [the longest x8 8.36 us: collect(): lax.dynamic_update_slice_in_dim(out, from_left, (place - step) % size * s...]
    all_gather x1, waiting for transfers between devices: 7.12 us -> 0.01 us  [body(): lax.all_gather(basis_in, 'blk', axis=2, tiled=True)]
    broadcast_in_dim x0 -> x1, local copies, waits for them, and re-layouts: none -> 3.06 us  [collect(): jnp.zeros((*value.shape[:dim], size * span, *value.shape[dim + 1:]), valu...]
  transfers between devices with their start and end apart: 3 -> 17, of which waited for: 3 -> 8; matrix products, arithmetic and copies ran while one was open for 9% -> 14% of each run, Pallas kernels for 0% -> 0%
where the time goes in v1:
time: 275 us
  waiting for transfers between devices  92.9 us (34%)
  blocking collectives  62.4 us (23%)
  matrix products  39.6 us (14%)
  local copies, waits for them, and re-layouts  29.5 us (11%)
  starting transfers between devices  29.5 us (11%)
  between operations  14 us (5%)
  other arithmetic  6.85 us (2%)
    all_gather x3, blocking collectives, body(): lax.all_gather((query_g, query_a, global_ids), 'blk', axis=1, tiled=True)  62.4 us
    all_gather x1, waiting for transfers between devices, body(): lax.all_gather(basis_out, 'blk', axis=2, tiled=True)  38.2 us
    ppermute x7, starting transfers between devices, collect(): from_right = lax.ppermute(from_right, axis, backward)  28.9 us
    ppermute x8, waiting for transfers between devices, collect(): from_left = lax.ppermute(from_left, axis, right)  28.7 us
    ppermute x7, waiting for transfers between devices, collect(): from_right = lax.ppermute(from_right, axis, backward)  24.6 us
    dot_general x4, matrix products, body(): jnp.einsum('ecn,ecf->enf', train_g * mask[:, :, None], train_a, preferred...  17.3 us
    dot_general x2, matrix products, turner(): jnp.einsum('ecd,edn->ecn', rows, piece, preferred_element_type=jnp.float32)  11 us
    dynamic_update_slice x8, local copies, waits for them, and re-layouts, collect(): lax.dynamic_update_slice_in_dim(out, from_left, (place - step) % size * s...  8.36 us
  transfers between devices with their start and end apart: 17, of which 8 were waited for; matrix products, arithmetic and copies ran while one was open for 14% of the time, Pallas kernels for 0%

profile of v1, /device:TPU:0, one launch (start us, length us, event | category | flops | bytes accessed | tf_op | source)
XLA Modules:
  0.0 274.8 jit_solution(12730324649266534088)
XLA Ops:
  8.5 5.1 %collective-permute-start.1 = (bf16[2,128,768]{2,1,0:T(8,128)(2,1)}, bf16[2,128,768]{2,1,0:T(8,128)(2,1)S(1)}, u32[]{:S(2)}, u32[]{:S(2)}) collective-permute-start(bf16[2,128,768]{2,1,0:T(8,128)(2,1)} %param.21), channel_id=1, source_target_pairs={{0,15},{1,0},{2,1},{3,2},{4,3},{5,4},{6,5},{7,6},{8,7},{9,8},{10,9... | collective-permute-start | bytes 1179656 | tf_op jit(solution)/shard_map/ppermute | solution.py:27
  21.7 1.3 gather_fusion.3
  23.0 1.6 gather_fusion.1
  24.7 4.5 %collective-permute-start.3 = (bf16[2,128,768]{2,1,0:T(8,128)(2,1)S(1)}, bf16[2,128,768]{2,1,0:T(8,128)(2,1)S(1)}, u32[]{:S(2)}, u32[]{:S(2)}) collective-permute-start(bf16[2,128,768]{2,1,0:T(8,128)(2,1)S(1)} %collective-permute-done.1), channel_id=1, source_target_pairs={{0,15},{1,0},{2,1},{3,2},{4,3},{5,4},{6,5},{7,6},{8,7},{9,8},{10,9... | collective-permute-start | bytes 1179656 | tf_op jit(solution)/shard_map/ppermute | solution.py:27
  29.2 6.9 %collective-permute-done.2 = bf16[2,128,768]{2,1,0:T(8,128)(2,1)S(1)} collective-permute-done((bf16[2,128,768]{2,1,0:T(8,128)(2,1)S(1)}, bf16[2,128,768]{2,1,0:T(8,128)(2,1)S(1)}, u32[]{:S(2)}, u32[]{:S(2)}) %collective-permute-start.2) | collective-permute-done | bytes 393248 | tf_op jit(solution)/shard_map/ppermute | solution.py:22
  36.1 4.5 %collective-permute-start.5 = (bf16[2,128,768]{2,1,0:T(8,128)(2,1)S(1)}, bf16[2,128,768]{2,1,0:T(8,128)(2,1)}, u32[]{:S(2)}, u32[]{:S(2)}) collective-permute-start(bf16[2,128,768]{2,1,0:T(8,128)(2,1)S(1)} %collective-permute-done.3), channel_id=1, source_target_pairs={{0,15},{1,0},{2,1},{3,2},{4,3},{5,4},{6,5},{7,6},{8,7},{9,8},{10,9... | collective-permute-start | bytes 1179656 | tf_op jit(solution)/shard_map/ppermute | solution.py:27
  41.6 9.9 %collective-permute-done.4 = bf16[2,128,768]{2,1,0:T(8,128)(2,1)S(1)} collective-permute-done((bf16[2,128,768]{2,1,0:T(8,128)(2,1)S(1)}, bf16[2,128,768]{2,1,0:T(8,128)(2,1)S(1)}, u32[]{:S(2)}, u32[]{:S(2)}) %collective-permute-start.4) | collective-permute-done | bytes 393248 | tf_op jit(solution)/shard_map/ppermute | solution.py:22
  52.8 4.5 %collective-permute-start.7 = (bf16[2,128,768]{2,1,0:T(8,128)(2,1)}, bf16[2,128,768]{2,1,0:T(8,128)(2,1)}, u32[]{:S(2)}, u32[]{:S(2)}) collective-permute-start(bf16[2,128,768]{2,1,0:T(8,128)(2,1)} %collective-permute-done.5), channel_id=1, source_target_pairs={{0,15},{1,0},{2,1},{3,2},{4,3},{5,4},{6,5},{7,6},{8,7},{9,8},{10,9... | collective-permute-start | bytes 1179656 | tf_op jit(solution)/shard_map/ppermute | solution.py:27
  57.5 7.2 %collective-permute-done.6 = bf16[2,128,768]{2,1,0:T(8,128)(2,1)} collective-permute-done((bf16[2,128,768]{2,1,0:T(8,128)(2,1)S(1)}, bf16[2,128,768]{2,1,0:T(8,128)(2,1)}, u32[]{:S(2)}, u32[]{:S(2)}) %collective-permute-start.6) | collective-permute-done | bytes 393248 | tf_op jit(solution)/shard_map/ppermute | solution.py:22
  67.9 18.0 %all-gather = s32[16,3,2]{1,2,0:T(2,128)S(1)} all-gather(s32[1,3,2]{1,2,0:T(2,128)S(1)} %bitcast.49), channel_id=1, replica_groups=mesh['groups'=2,'blk'=16] {'blk'}, dimensions={0}, use_global_device_ids=true | all-gather | bytes 408 | tf_op jit(solution)/shard_map/all_gather | solution.py:96
  86.1 3.1 %broadcast_in_dim.8 = bf16[2,2048,768]{2,1,0:T(8,128)(2,1)} broadcast(bf16[]{:T(256)} %constant.128.clone.1), dimensions={} | broadcast | bytes 6291458 | tf_op jit(solution)/shard_map/broadcast_in_dim | solution.py:17
  95.1 10.8 %collective-permute-done.9 = bf16[2,128,768]{2,1,0:T(8,128)(2,1)S(1)} collective-permute-done((bf16[2,128,768]{2,1,0:T(8,128)(2,1)}, bf16[2,128,768]{2,1,0:T(8,128)(2,1)S(1)}, u32[]{:S(2)}, u32[]{:S(2)}) %collective-permute-start.9) | collective-permute-done | bytes 393248 | tf_op jit(solution)/shard_map/ppermute | solution.py:27
  105.9 4.5 %collective-permute-start.11 = (bf16[2,128,768]{2,1,0:T(8,128)(2,1)S(1)}, bf16[2,128,768]{2,1,0:T(8,128)(2,1)S(1)}, u32[]{:S(2)}, u32[]{:S(2)}) collective-permute-start(bf16[2,128,768]{2,1,0:T(8,128)(2,1)S(1)} %collective-permute-done.9), channel_id=1, source_target_pairs={{0,15},{1,0},{2,1},{3,2},{4,3},{5,4},{6,5},{7,6},{8,7},{9,8},{10,9... | collective-permute-start | bytes 1179656 | tf_op jit(solution)/shard_map/ppermute | solution.py:27
  110.4 1.8 constant_dynamic-update-slice_fusion.9
  112.2 1.8 constant_dynamic-update-slice_fusion.8
  114.0 1.8 constant_dynamic-update-slice_fusion.7
  115.8 1.8 constant_dynamic-update-slice_fusion.6
  117.6 3.6 %collective-permute-done.11 = bf16[2,128,768]{2,1,0:T(8,128)(2,1)S(1)} collective-permute-done((bf16[2,128,768]{2,1,0:T(8,128)(2,1)S(1)}, bf16[2,128,768]{2,1,0:T(8,128)(2,1)S(1)}, u32[]{:S(2)}, u32[]{:S(2)}) %collective-permute-start.11) | collective-permute-done | bytes 393248 | tf_op jit(solution)/shard_map/ppermute | solution.py:27
  121.2 4.7 %collective-permute-start.13 = (bf16[2,128,768]{2,1,0:T(8,128)(2,1)S(1)}, bf16[2,128,768]{2,1,0:T(8,128)(2,1)S(1)}, u32[]{:S(2)}, u32[]{:S(2)}) collective-permute-start(bf16[2,128,768]{2,1,0:T(8,128)(2,1)S(1)} %collective-permute-done.11), channel_id=1, source_target_pairs={{0,15},{1,0},{2,1},{3,2},{4,3},{5,4},{6,5},{7,6},{8,7},{9,8},{10,9... | collective-permute-start | bytes 1179656 | tf_op jit(solution)/shard_map/ppermute | solution.py:27
  129.1 10.2 %collective-permute-done.13 = bf16[2,128,768]{2,1,0:T(8,128)(2,1)S(1)} collective-permute-done((bf16[2,128,768]{2,1,0:T(8,128)(2,1)S(1)}, bf16[2,128,768]{2,1,0:T(8,128)(2,1)S(1)}, u32[]{:S(2)}, u32[]{:S(2)}) %collective-permute-start.13) | collective-permute-done | bytes 393248 | tf_op jit(solution)/shard_map/ppermute | solution.py:27
  140.1 4.7 %collective-permute-done.14 = bf16[2,128,768]{2,1,0:T(8,128)(2,1)S(1)} collective-permute-done((bf16[2,128,768]{2,1,0:T(8,128)(2,1)S(1)}, bf16[2,128,768]{2,1,0:T(8,128)(2,1)S(1)}, u32[]{:S(2)}, u32[]{:S(2)}) %collective-permute-start.14) | collective-permute-done | bytes 393248 | tf_op jit(solution)/shard_map/ppermute | solution.py:22
  145.6 2.6 convolution_convert_fusion.1
  148.2 23.5 %all_gather.17 = bf16[2,48,768]{2,0,1:T(2,128)(2,1)S(1)} all-gather(bf16[2,3,768]{2,0,1:T(2,128)(2,1)S(1)} %copy.20), channel_id=1, replica_groups=mesh['groups'=2,'blk'=16] {'blk'}, dimensions={1}, use_global_device_ids=true | all-gather | bytes 156672 | tf_op jit(solution)/shard_map/all_gather | solution.py:96
  171.7 38.2 %all-gather.4.cloned.1.call-done = bf16[2,2048,2048]{2,1,0:T(8,128)(2,1)} async-done(((bf16[2,2048,128]{2,1,0:T(8,128)(2,1)}), bf16[2,2048,2048]{2,1,0:T(8,128)(2,1)}) %all-gather.4.cloned.1.call-update) | async-done | bytes 16777232 | tf_op jit(solution)/shard_map/all_gather | solution.py:77
  209.9 8.5 %convolution_convert_fusion = bf16[2,99,2048]{2,1,0:T(8,128)(2,1)S(1)} fusion(bf16[2,2048,2048]{2,1,0:T(8,128)(2,1)} %all-gather.4.cloned.1.call-done, bf16[2,99,2048]{2,1,0:T(8,128)(2,1)S(1)} %reshape.209, bf16[2,99]{1,0:T(2,128)(2,1)S(1)} %pad_maximum_fusion.3), kind=kOutput, calls=%fused_computation.23 | convolution fusion | flops 1661755392 | bytes 18399628 | tf_op jit(solution)/shard_map/ecd,edn->ecn/dot_general | solution.py:48
  218.4 4.3 %fusion.3 = bf16[1,2,2048,768]{3,2,1,0:T(8,128)(2,1)S(1)} fusion(bf16[2,2048,768]{2,1,0:T(8,128)(2,1)} %constant_dynamic-update-slice_fusion, bf16[2,99,2048]{2,1,0:T(8,128)(2,1)S(1)} %convolution_convert_fusion, bf16[2,96]{1,0:T(2,128)(2,1)S(1)} %reshape.293, bf16[2,99,768]{2,1,0:T(8,128)(2,1)S(1)} %convolution_convert_fusion.1), kind=kOutput, calls=%fused_computation.17 | convolution fusion | flops 616955904 | bytes 13664768 | tf_op jit(solution)/shard_map/ecn,ecf->enf/dot_general | solution.py:91
  222.7 4.3 %fusion.4 = bf16[1,2,2048,768]{3,2,1,0:T(8,128)(2,1)S(1)} fusion(bf16[2,2048,768]{2,1,0:T(8,128)(2,1)} %constant_dynamic-update-slice_fusion, bf16[2,99,2048]{2,1,0:T(8,128)(2,1)S(1)} %convolution_convert_fusion, bf16[2,96]{1,0:T(2,128)(2,1)S(1)} %reshape.294, bf16[2,99,768]{2,1,0:T(8,128)(2,1)S(1)} %convolution_convert_fusion.1), kind=kOutput, calls=%fused_computation.18 | convolution fusion | flops 616955904 | bytes 13664768 | tf_op jit(solution)/shard_map/ecn,ecf->enf/dot_general | solution.py:91
  227.0 4.3 %fusion.2 = bf16[1,2,2048,768]{3,2,1,0:T(8,128)(2,1)S(1)} fusion(bf16[2,2048,768]{2,1,0:T(8,128)(2,1)} %constant_dynamic-update-slice_fusion, bf16[2,99,2048]{2,1,0:T(8,128)(2,1)S(1)} %convolution_convert_fusion, bf16[2,96]{1,0:T(2,128)(2,1)S(1)} %reshape.292, bf16[2,99,768]{2,1,0:T(8,128)(2,1)S(1)} %convolution_convert_fusion.1), kind=kOutput, calls=%fused_computation.16 | convolution fusion | flops 616955904 | bytes 13664768 | tf_op jit(solution)/shard_map/ecn,ecf->enf/dot_general | solution.py:91
  231.3 4.3 %fusion.5 = bf16[1,2,2048,768]{3,2,1,0:T(8,128)(2,1)S(1)} fusion(bf16[2,2048,768]{2,1,0:T(8,128)(2,1)} %constant_dynamic-update-slice_fusion, bf16[2,99,2048]{2,1,0:T(8,128)(2,1)S(1)} %convolution_convert_fusion, bf16[2,96]{1,0:T(2,128)(2,1)S(1)} %reshape.295, bf16[2,99,768]{2,1,0:T(8,128)(2,1)S(1)} %convolution_convert_fusion.1), kind=kOutput, calls=%fused_computation.19 | convolution fusion | flops 616955904 | bytes 13664768 | tf_op jit(solution)/shard_map/ecn,ecf->enf/dot_general | solution.py:91
  235.7 20.9 %all_gather.18 = bf16[2,48,2048]{2,0,1:T(2,128)(2,1)S(1)} all-gather(bf16[2,3,2048]{2,0,1:T(2,128)(2,1)S(1)} %copy.23), channel_id=1, replica_groups=mesh['groups'=2,'blk'=16] {'blk'}, dimensions={1}, use_global_device_ids=true | all-gather | bytes 417792 | tf_op jit(solution)/shard_map/all_gather | solution.py:96
  256.6 8.4 %fusion.8 = bf16[4,2,48,2048]{3,2,0,1:T(8,128)(2,1)S(1)} fusion(bf16[2,48,768,1]{2,0,1,3:T(2,128)(2,1)S(1)} %bitcast.46, bf16[1,2,2048,768]{3,2,1,0:T(8,128)(2,1)S(1)} %fusion.5, bf16[1,2,2048,768]{3,2,1,0:T(8,128)(2,1)S(1)} %fusion.4, bf16[1,2,2048,768]{3,2,1,0:T(8,128)(2,1)S(1)} %fusion.3, bf16[1,2,2048,768]{3,2,1,0:T(8,128)(2,1)S(1)} %fusion.2), kind=kOutput, calls=%fused_computation.22 | convolution fusion | flops 1245708288 | bytes 26886144 | tf_op jit(solution)/shard_map/esf,kedf->kesd/dot_general | solution.py:99
  264.9 2.2 fusion.6
  (105 shorter events, 27.3 us)
Async XLA Ops:
  6.5 16.5 %copy-start = (s32[128]{0:T(128)S(1)}, s32[128]{0:T(128)}, u32[]{:S(2)}) copy-start(s32[128]{0:T(128)} %param.14) | copy-start | bytes 1540
  6.5 139.0 %all-gather.6.cloned.1.call-start = ((), (), s32[]{:S(2)}) async-start(), calls=%async_computation.1 | async-start | bytes 2506752 | tf_op jit(solution)/shard_map/all_gather | solution.py:78
  7.3 202.6 %all-gather.4.cloned.1.call-start = ((), (), s32[]{:S(2)}) async-start(), calls=%async_computation | async-start | bytes 17825792 | tf_op jit(solution)/shard_map/all_gather | solution.py:77
  8.0 16.6 %collective-permute-start = (bf16[2,128,768]{2,1,0:T(8,128)(2,1)}, bf16[2,128,768]{2,1,0:T(8,128)(2,1)S(1)}, u32[]{:S(2)}, u32[]{:S(2)}) collective-permute-start(bf16[2,128,768]{2,1,0:T(8,128)(2,1)} %param.21), channel_id=1, source_target_pairs={{0,1},{1,2},{2,3},{3,4},{4,5},{5,6},{6,7},{7,8},{8,9},{9,10},{10,1... | collective-permute-start | bytes 1179656 | tf_op jit(solution)/shard_map/ppermute | solution.py:22
  8.5 16.2 %collective-permute-start.1 = (bf16[2,128,768]{2,1,0:T(8,128)(2,1)}, bf16[2,128,768]{2,1,0:T(8,128)(2,1)S(1)}, u32[]{:S(2)}, u32[]{:S(2)}) collective-permute-start(bf16[2,128,768]{2,1,0:T(8,128)(2,1)} %param.21), channel_id=1, source_target_pairs={{0,15},{1,0},{2,1},{3,2},{4,3},{5,4},{6,5},{7,6},{8,7},{9,8},{10,9... | collective-permute-start | bytes 1179656 | tf_op jit(solution)/shard_map/ppermute | solution.py:27
  24.6 11.5 %copy-start.2 = (bf16[2,128,768]{2,1,0:T(8,128)(2,1)}, bf16[2,128,768]{2,1,0:T(8,128)(2,1)S(1)}, u32[]{:S(2)}) copy-start(bf16[2,128,768]{2,1,0:T(8,128)(2,1)S(1)} %collective-permute-done) | copy-start | bytes 1179652
  24.6 11.4 %collective-permute-start.2 = (bf16[2,128,768]{2,1,0:T(8,128)(2,1)S(1)}, bf16[2,128,768]{2,1,0:T(8,128)(2,1)S(1)}, u32[]{:S(2)}, u32[]{:S(2)}) collective-permute-start(bf16[2,128,768]{2,1,0:T(8,128)(2,1)S(1)} %collective-permute-done), channel_id=1, source_target_pairs={{0,1},{1,2},{2,3},{3,4},{4,5},{5,6},{6,7},{7,8},{8,9},{9,10},{10,1... | collective-permute-start | bytes 1179656 | tf_op jit(solution)/shard_map/ppermute | solution.py:22
  24.7 11.3 %collective-permute-start.3 = (bf16[2,128,768]{2,1,0:T(8,128)(2,1)S(1)}, bf16[2,128,768]{2,1,0:T(8,128)(2,1)S(1)}, u32[]{:S(2)}, u32[]{:S(2)}) collective-permute-start(bf16[2,128,768]{2,1,0:T(8,128)(2,1)S(1)} %collective-permute-done.1), channel_id=1, source_target_pairs={{0,15},{1,0},{2,1},{3,2},{4,3},{5,4},{6,5},{7,6},{8,7},{9,8},{10,9... | collective-permute-start | bytes 1179656 | tf_op jit(solution)/shard_map/ppermute | solution.py:27
  36.0 15.5 %collective-permute-start.4 = (bf16[2,128,768]{2,1,0:T(8,128)(2,1)S(1)}, bf16[2,128,768]{2,1,0:T(8,128)(2,1)S(1)}, u32[]{:S(2)}, u32[]{:S(2)}) collective-permute-start(bf16[2,128,768]{2,1,0:T(8,128)(2,1)S(1)} %collective-permute-done.2), channel_id=1, source_target_pairs={{0,1},{1,2},{2,3},{3,4},{4,5},{5,6},{6,7},{7,8},{8,9},{9,10},{10,1... | collective-permute-start | bytes 1179656 | tf_op jit(solution)/shard_map/ppermute | solution.py:22
  36.1 28.9 %copy-start.4 = (bf16[2,128,768]{2,1,0:T(8,128)(2,1)}, bf16[2,128,768]{2,1,0:T(8,128)(2,1)S(1)}, u32[]{:S(2)}) copy-start(bf16[2,128,768]{2,1,0:T(8,128)(2,1)S(1)} %collective-permute-done.3) | copy-start | bytes 1179652
  36.1 16.7 %collective-permute-start.5 = (bf16[2,128,768]{2,1,0:T(8,128)(2,1)S(1)}, bf16[2,128,768]{2,1,0:T(8,128)(2,1)}, u32[]{:S(2)}, u32[]{:S(2)}) collective-permute-start(bf16[2,128,768]{2,1,0:T(8,128)(2,1)S(1)} %collective-permute-done.3), channel_id=1, source_target_pairs={{0,15},{1,0},{2,1},{3,2},{4,3},{5,4},{6,5},{7,6},{8,7},{9,8},{10,9... | collective-permute-start | bytes 1179656 | tf_op jit(solution)/shard_map/ppermute | solution.py:27
  51.5 13.5 %copy-start.6 = (bf16[2,128,768]{2,1,0:T(8,128)(2,1)}, bf16[2,128,768]{2,1,0:T(8,128)(2,1)S(1)}, u32[]{:S(2)}) copy-start(bf16[2,128,768]{2,1,0:T(8,128)(2,1)S(1)} %collective-permute-done.4) | copy-start | bytes 1179652
  51.5 13.2 %collective-permute-start.6 = (bf16[2,128,768]{2,1,0:T(8,128)(2,1)S(1)}, bf16[2,128,768]{2,1,0:T(8,128)(2,1)}, u32[]{:S(2)}, u32[]{:S(2)}) collective-permute-start(bf16[2,128,768]{2,1,0:T(8,128)(2,1)S(1)} %collective-permute-done.4), channel_id=1, source_target_pairs={{0,1},{1,2},{2,3},{3,4},{4,5},{5,6},{6,7},{7,8},{8,9},{9,10},{10,1... | collective-permute-start | bytes 1179656 | tf_op jit(solution)/shard_map/ppermute | solution.py:22
  52.8 38.0 %collective-permute-start.7 = (bf16[2,128,768]{2,1,0:T(8,128)(2,1)}, bf16[2,128,768]{2,1,0:T(8,128)(2,1)}, u32[]{:S(2)}, u32[]{:S(2)}) collective-permute-start(bf16[2,128,768]{2,1,0:T(8,128)(2,1)} %collective-permute-done.5), channel_id=1, source_target_pairs={{0,15},{1,0},{2,1},{3,2},{4,3},{5,4},{6,5},{7,6},{8,7},{9,8},{10,9... | collective-permute-start | bytes 1179656 | tf_op jit(solution)/shard_map/ppermute | solution.py:27
  64.7 28.0 %collective-permute-start.8 = (bf16[2,128,768]{2,1,0:T(8,128)(2,1)}, bf16[2,128,768]{2,1,0:T(8,128)(2,1)}, u32[]{:S(2)}, u32[]{:S(2)}) collective-permute-start(bf16[2,128,768]{2,1,0:T(8,128)(2,1)} %collective-permute-done.6), channel_id=1, source_target_pairs={{0,1},{1,2},{2,3},{3,4},{4,5},{5,6},{6,7},{7,8},{8,9},{9,10},{10,1... | collective-permute-start | bytes 1179656 | tf_op jit(solution)/shard_map/ppermute | solution.py:22
  66.1 23.1 %copy-start.1 = (bf16[2,128,768]{2,1,0:T(8,128)(2,1)S(1)}, bf16[2,128,768]{2,1,0:T(8,128)(2,1)}, u32[]{:S(2)}) copy-start(bf16[2,128,768]{2,1,0:T(8,128)(2,1)} %param.21) | copy-start | bytes 1179652
  66.3 23.6 %copy-start.3 = (bf16[2,128,768]{2,1,0:T(8,128)(2,1)S(1)}, bf16[2,128,768]{2,1,0:T(8,128)(2,1)}, u32[]{:S(2)}) copy-start(bf16[2,128,768]{2,1,0:T(8,128)(2,1)} %copy-done.2) | copy-start | bytes 1179652
  66.3 27.1 %copy-start.5 = (bf16[2,128,768]{2,1,0:T(8,128)(2,1)S(1)}, bf16[2,128,768]{2,1,0:T(8,128)(2,1)}, u32[]{:S(2)}) copy-start(bf16[2,128,768]{2,1,0:T(8,128)(2,1)} %copy-done.4) | copy-start | bytes 1179652
  86.1 8.1 %copy-start.7 = (bf16[2,128,768]{2,1,0:T(8,128)(2,1)S(1)}, bf16[2,128,768]{2,1,0:T(8,128)(2,1)}, u32[]{:S(2)}) copy-start(bf16[2,128,768]{2,1,0:T(8,128)(2,1)} %copy-done.6) | copy-start | bytes 1179652
  90.8 15.1 %collective-permute-start.9 = (bf16[2,128,768]{2,1,0:T(8,128)(2,1)}, bf16[2,128,768]{2,1,0:T(8,128)(2,1)S(1)}, u32[]{:S(2)}, u32[]{:S(2)}) collective-permute-start(bf16[2,128,768]{2,1,0:T(8,128)(2,1)} %collective-permute-done.7), channel_id=1, source_target_pairs={{0,15},{1,0},{2,1},{3,2},{4,3},{5,4},{6,5},{7,6},{8,7},{9,8},{10,9... | collective-permute-start | bytes 1179656 | tf_op jit(solution)/shard_map/ppermute | solution.py:27
  92.7 19.5 %collective-permute-start.10 = (bf16[2,128,768]{2,1,0:T(8,128)(2,1)}, bf16[2,128,768]{2,1,0:T(8,128)(2,1)S(1)}, u32[]{:S(2)}, u32[]{:S(2)}) collective-permute-start(bf16[2,128,768]{2,1,0:T(8,128)(2,1)} %collective-permute-done.8), channel_id=1, source_target_pairs={{0,1},{1,2},{2,3},{3,4},{4,5},{5,6},{6,7},{7,8},{8,9},{9,10},{10,1... | collective-permute-start | bytes 1179656 | tf_op jit(solution)/shard_map/ppermute | solution.py:22
  105.9 15.3 %collective-permute-start.11 = (bf16[2,128,768]{2,1,0:T(8,128)(2,1)S(1)}, bf16[2,128,768]{2,1,0:T(8,128)(2,1)S(1)}, u32[]{:S(2)}, u32[]{:S(2)}) collective-permute-start(bf16[2,128,768]{2,1,0:T(8,128)(2,1)S(1)} %collective-permute-done.9), channel_id=1, source_target_pairs={{0,15},{1,0},{2,1},{3,2},{4,3},{5,4},{6,5},{7,6},{8,7},{9,8},{10,9... | collective-permute-start | bytes 1179656 | tf_op jit(solution)/shard_map/ppermute | solution.py:27
  112.2 14.4 %collective-permute-start.12 = (bf16[2,128,768]{2,1,0:T(8,128)(2,1)S(1)}, bf16[2,128,768]{2,1,0:T(8,128)(2,1)S(1)}, u32[]{:S(2)}, u32[]{:S(2)}) collective-permute-start(bf16[2,128,768]{2,1,0:T(8,128)(2,1)S(1)} %collective-permute-done.10), channel_id=1, source_target_pairs={{0,1},{1,2},{2,3},{3,4},{4,5},{5,6},{6,7},{7,8},{8,9},{9,10},{10,1... | collective-permute-start | bytes 1179656 | tf_op jit(solution)/shard_map/ppermute | solution.py:22
  121.2 18.1 %collective-permute-start.13 = (bf16[2,128,768]{2,1,0:T(8,128)(2,1)S(1)}, bf16[2,128,768]{2,1,0:T(8,128)(2,1)S(1)}, u32[]{:S(2)}, u32[]{:S(2)}) collective-permute-start(bf16[2,128,768]{2,1,0:T(8,128)(2,1)S(1)} %collective-permute-done.11), channel_id=1, source_target_pairs={{0,15},{1,0},{2,1},{3,2},{4,3},{5,4},{6,5},{7,6},{8,7},{9,8},{10,9... | collective-permute-start | bytes 1179656 | tf_op jit(solution)/shard_map/ppermute | solution.py:27
  126.6 18.1 %collective-permute-start.14 = (bf16[2,128,768]{2,1,0:T(8,128)(2,1)S(1)}, bf16[2,128,768]{2,1,0:T(8,128)(2,1)S(1)}, u32[]{:S(2)}, u32[]{:S(2)}) collective-permute-start(bf16[2,128,768]{2,1,0:T(8,128)(2,1)S(1)} %collective-permute-done.12), channel_id=1, source_target_pairs={{0,1},{1,2},{2,3},{3,4},{4,5},{5,6},{6,7},{7,8},{8,9},{9,10},{10,1... | collective-permute-start | bytes 1179656 | tf_op jit(solution)/shard_map/ppermute | solution.py:22
Sparse Core Ops, SparseCore 0:
  9.6 53.8 all-gather.5
  65.7 144.1 all-gather.3
